TPU v7x, 32 devices: a whole 2x2x4 slice. The times are simulated.
32 devices in a mesh: tile: 8 (over z, y), segment: 4 (over x, core).
Axes of the slice: x: 2, y: 2, z: 4, core: 2. Of those that a mesh axis runs over, the one named last changes fastest.
Arguments:
- cube: float32 [16, 96, 1024], P(None, 'tile'), may hold values from -6 to 6
- footprint: int32 [16, 1024], replicated, may hold values 0 or 1
- lift_weight: float32 [32], replicated, may hold values from -4 to 4
- lift_bias: float32 [32], replicated, may hold values from -2 to 2
- spatial_weight: bfloat16 [8, 32, 288], P('segment'), may hold values from -0.375 to 0.375
- spatial_bias: bfloat16 [8, 32], P('segment'), may hold values from -2 to 2
- spectral_weight: bfloat16 [8, 32, 96], P('segment'), may hold values from -1.5 to 1.5
- head_weight: float32 [32], replicated, may hold values from -1 to 1
Outputs:
- scores: float32 [16, 96, 1024], P('segment', 'tile')
All inputs are finite; a program needn't handle non-finite values.
Results may differ from a plain program's by a relative error of at most 0.035.
Values may be sent and summed in bfloat16 or wider, within the bound.
A program may use at most 64 MiB of HBM per device.

v0:
```python
import jax
import jax.numpy as jnp
from jax import lax
from jax.sharding import PartitionSpec as P

SKY = 32


def extended(block, sides, width):
    for axis, dim in sides:
        count = lax.axis_size(axis)
        forward = [(i, i + 1) for i in range(count - 1)]
        backward = [(target, source) for source, target in forward]
        low = lax.ppermute(
            lax.slice_in_dim(block, block.shape[dim] - width, None, axis=dim), axis, forward
        )
        high = lax.ppermute(lax.slice_in_dim(block, 0, width, axis=dim), axis, backward)
        block = jnp.concatenate([low, block, high], axis=dim)
    return block


def spatial_part(field, weight, bias_row):
    pixels = field.shape[2]
    column = jnp.arange(pixels) % SKY
    padded = jnp.pad(field, ((0, 0), (0, 0), (SKY + 1, SKY + 1)))
    windows = []
    for row_step in (-1, 0, 1):
        for col_step in (-1, 0, 1):
            offset = SKY + 1 + row_step * SKY + col_step
            window = padded[:, :, offset : offset + pixels]
            if col_step != 0:
                inside = ((column + col_step >= 0) & (column + col_step < SKY)).astype(field.dtype)
                window = window * inside[None, None, :]
            windows.append(window)
    stacked = jnp.concatenate(windows, axis=1)
    summed = jnp.einsum("oi,nip->nop", weight, stacked, preferred_element_type=jnp.float32)
    return jax.nn.silu(summed + bias_row.astype(jnp.float32)[None, :, None])


def spectral_mix(weight, rimmed, count):
    width = weight.shape[0]
    mixed = jnp.einsum(
        "oi,nip->nop", weight[:, 0:width], rimmed[0:count], preferred_element_type=jnp.float32
    )
    mixed = mixed + jnp.einsum(
        "oi,nip->nop",
        weight[:, width : 2 * width],
        rimmed[1 : count + 1],
        preferred_element_type=jnp.float32,
    )
    return mixed + jnp.einsum(
        "oi,nip->nop",
        weight[:, 2 * width : 3 * width],
        rimmed[2 : count + 2],
        preferred_element_type=jnp.float32,
    )


def run_section(field, spatial_w, spatial_b, spectral_w, keep_mask):
    depth = spatial_w.shape[0]
    planes = field.shape[0]
    keep_wide = keep_mask[None, None, :]
    for layer in range(depth):
        gated = spatial_part(field, spatial_w[layer], spatial_b[layer]).astype(jnp.bfloat16)
        rimmed = extended(gated, (("tile", 0),), 1)
        mixed = spectral_mix(spectral_w[layer], rimmed, planes)
        field = (keep_wide * (0.5 * field.astype(jnp.float32) + mixed)).astype(jnp.bfloat16)
    return field


def per_device(
    cube,
    footprint,
    lift_weight,
    lift_bias,
    spatial_weight,
    spatial_bias,
    spectral_weight,
    head_weight,
):
    micro = cube.shape[0]
    planes = cube.shape[1]
    pixels = cube.shape[2]
    segments = lax.axis_size("segment")
    segment_id = lax.axis_index("segment")

    def lift_cube(micro_id):
        plane = lax.dynamic_index_in_dim(cube, micro_id, 0, keepdims=False)
        keep_mask = lax.dynamic_index_in_dim(footprint, micro_id, 0, keepdims=False).astype(
            jnp.float32
        )
        fresh = keep_mask[None, None, :] * (
            lift_weight[None, :, None] * plane[:, None, :] + lift_bias[None, :, None]
        )
        return (fresh.astype(jnp.bfloat16), keep_mask)

    def score_head(field):
        return jnp.einsum(
            "c,fcp->fp", head_weight, field.astype(jnp.float32), precision=lax.Precision.HIGHEST
        )

    all_spatial, all_bias, all_spectral = (
        lax.all_gather(spatial_weight, "segment", axis=0, tiled=True),
        lax.all_gather(spatial_bias, "segment", axis=0, tiled=True),
        lax.all_gather(spectral_weight, "segment", axis=0, tiled=True),
    )
    depth = spatial_weight.shape[0]
    owned = micro // segments

    def one_field(within, results):
        fresh, keep_mask = lift_cube(segment_id * owned + within)

        def section_step(section, field):
            spatial_w = lax.dynamic_slice_in_dim(all_spatial, section * depth, depth, 0)
            spatial_b = lax.dynamic_slice_in_dim(all_bias, section * depth, depth, 0)
            spectral_w = lax.dynamic_slice_in_dim(all_spectral, section * depth, depth, 0)
            return run_section(field, spatial_w, spatial_b, spectral_w, keep_mask)

        field = lax.fori_loop(0, segments, section_step, fresh)
        return lax.dynamic_update_index_in_dim(results, score_head(field), within, 0)

    return lax.fori_loop(0, owned, one_field, jnp.zeros((owned, planes, pixels), jnp.float32))


def solution(mesh):
    placed = (
        P(None, "tile", None),
        P(),
        P(),
        P(),
        P("segment", None, None),
        P("segment", None),
        P("segment", None, None),
        P(),
    )
    return jax.shard_map(
        per_device,
        mesh=mesh,
        in_specs=placed,
        out_specs=P("segment", "tile", None),
        check_vma=False,
    )
```

profile of v0, /device:TPU:0, one launch (start us, length us, event | category | flops | bytes accessed | tf_op | source)
XLA Modules:
  0.0 699.4 jit_solution(17412912206498630684)
XLA Ops:
  0.0 7.0 %all_gather.9 = bf16[8,32,288]{2,1,0:T(8,128)(2,1)S(1)} all-gather(bf16[2,32,288]{2,1,0:T(8,128)(2,1)} %param.16), channel_id=1, replica_groups=mesh['tile'=8,'segment'=4] {'segment'}, dimensions={0}, use_global_device_ids=true | all-gather | bytes 184320 | tf_op jit(solution)/shard_map/all_gather | solution.py:103
  7.0 5.4 all_gather.11
  12.5 5.2 all-gather
  17.6 681.8 %while.49 = (s32[]{:T(128)}, f32[4,12,1024]{2,0,1:T(4,128)}, s32[]{:T(128)}, s32[16,1024]{1,0:T(8,128)}, f32[32]{0:T(128)}, /*index=5*/f32[16,12,1024]{2,0,1:T(8...) while((s32[]{:T(128)}, f32[4,12,1024]{2,0,1:T(4,128)}, ...), condition=%wide.region_3.4_spmd, body=%wide.region_0.3_spmd.sunk | while | flops 645684288 | bytes 69631216 | solution.py:122
  20.4 170.2 %while.50 = (s32[]{:T(128)}, bf16[12,32,1024]{2,1,0:T(8,128)(2,1)S(1)}, f32[1024]{0:T(1024)S(1)}, bf16[8,32,288]{2,1,0:T(8,128)(2,1)S(1)}, bf16[8,32]{1,0:T(8,12...) while((s32[]{:T(128)}, ...), condition=%wide.region_2.2_spmd, body=%wide.region_1.1_spmd.sunk | while | flops 639391808 | bytes 67651600 | solution.py:119
  32.1 4.5 fusion.78
  75.2 4.5 fusion.78
  101.4 4.3 collective-permute-done.3
  118.1 4.5 fusion.78
  161.0 4.5 fusion.78
  185.7 4.3 collective-permute-done.3
  195.9 163.8 %while.50 = (s32[]{:T(128)}, bf16[12,32,1024]{2,1,0:T(8,128)(2,1)S(1)}, f32[1024]{0:T(1024)S(1)}, bf16[8,32,288]{2,1,0:T(8,128)(2,1)S(1)}, bf16[8,32]{1,0:T(8,12...) while((s32[]{:T(128)}, ...), condition=%wide.region_2.2_spmd, body=%wide.region_1.1_spmd.sunk | while | flops 639391808 | bytes 67651600 | solution.py:119
  207.6 4.5 fusion.78
  248.3 4.5 fusion.78
  273.2 4.3 collective-permute-done.3
  289.8 4.5 fusion.78
  330.6 4.5 fusion.78
  354.7 4.4 collective-permute-done.3
  365.0 163.1 %while.50 = (s32[]{:T(128)}, bf16[12,32,1024]{2,1,0:T(8,128)(2,1)S(1)}, f32[1024]{0:T(1024)S(1)}, bf16[8,32,288]{2,1,0:T(8,128)(2,1)S(1)}, bf16[8,32]{1,0:T(8,12...) while((s32[]{:T(128)}, ...), condition=%wide.region_2.2_spmd, body=%wide.region_1.1_spmd.sunk | while | flops 639391808 | bytes 67651600 | solution.py:119
  376.6 4.5 fusion.78
  417.4 4.5 fusion.78
  441.5 4.6 collective-permute-done.3
  458.5 4.5 fusion.78
  482.3 4.4 collective-permute-done.3
  499.0 4.5 fusion.78
  533.3 163.7 %while.50 = (s32[]{:T(128)}, bf16[12,32,1024]{2,1,0:T(8,128)(2,1)S(1)}, f32[1024]{0:T(1024)S(1)}, bf16[8,32,288]{2,1,0:T(8,128)(2,1)S(1)}, bf16[8,32]{1,0:T(8,12...) while((s32[]{:T(128)}, ...), condition=%wide.region_2.2_spmd, body=%wide.region_1.1_spmd.sunk | while | flops 639391808 | bytes 67651600 | solution.py:119
  545.0 4.5 fusion.78
  586.2 4.5 fusion.78
  610.3 4.4 collective-permute-done.3
  627.0 4.5 fusion.78
  667.8 4.5 fusion.78
  692.0 4.3 collective-permute-done.3
  (729 shorter events, 571.8 us)
Async XLA Ops:
  40.2 6.2 collective-permute-start.1
  52.0 6.2 collective-permute-start.2
  56.7 6.2 collective-permute-start.3
  83.1 6.2 collective-permute-start.1
  94.8 6.2 collective-permute-start.2
  99.6 6.2 collective-permute-start.3
  126.0 6.2 collective-permute-start.1
  137.7 6.2 collective-permute-start.2
  142.5 6.2 collective-permute-start.3
  168.9 6.2 collective-permute-start.1
  183.9 6.2 collective-permute-start.3
  214.9 6.2 collective-permute-start.1
  229.9 6.2 collective-permute-start.3
  256.4 6.2 collective-permute-start.1
  271.3 6.2 collective-permute-start.3
  297.1 6.2 collective-permute-start.1
  312.1 6.2 collective-permute-start.3
  337.9 6.2 collective-permute-start.1
  352.9 6.2 collective-permute-start.3
  383.9 6.2 collective-permute-start.1
  398.9 6.2 collective-permute-start.3
  424.7 6.2 collective-permute-start.1
  439.7 6.4 collective-permute-start.3
  465.5 6.2 collective-permute-start.1
  480.5 6.2 collective-permute-start.3
  552.3 6.2 collective-permute-start.1
  567.8 6.2 collective-permute-start.3
  593.5 6.2 collective-permute-start.1
  608.5 6.2 collective-permute-start.3
  634.3 6.2 collective-permute-start.1
  675.2 6.2 collective-permute-start.1
  690.2 6.2 collective-permute-start.3
  (68 other events, 1020.9 us)
where the time goes:
time: 703 us; the launch traced here: 699 us
  other arithmetic  177 us (25%)
  matrix products  141 us (20%)
  starting transfers between devices  140 us (20%)
  waiting for transfers between devices  138 us (20%)
  local copies, waits for them, and re-layouts  82.6 us (12%)
  blocking collectives  17.6 us (3%)
    while x160, other arithmetic  141 us
    ppermute x32, waiting for transfers between devices, extended(): lax.ppermute(lax.slice_in_dim(block, 0, width, axis=dim), axis, backward)  133 us
    ppermute x32, starting transfers between devices, extended(): lax.ppermute(lax.slice_in_dim(block, block.shape[dim] - width, None, axis...  98.5 us
    dot_general x32, matrix products, spatial_part(): jnp.einsum('oi,nip->nop', weight, stacked, preferred_element_type=jnp.flo...  94.6 us
    while x168, local copies, waits for them, and re-layouts  70.1 us
    ppermute x32, starting transfers between devices, extended(): lax.ppermute(lax.slice_in_dim(block, 0, width, axis=dim), axis, backward)  41.3 us
    concatenate x32, other arithmetic, spatial_part(): stacked = jnp.concatenate(windows, axis=1)  28.6 us
    dot_general x32, matrix products, spectral_mix(): jnp.einsum('oi,nip->nop', weight[:, 2 * width:3 * width], rimmed[2:count...  20.4 us
  transfers between devices with their start and end apart: 64, of which 64 were waited for; matrix products, arithmetic and copies ran while one was open for 3% of the time, Pallas kernels for 0%

commit v1 on v0

v1 whole, which is shorter than its diff:
```python
import functools

import jax
import jax.numpy as jnp
from jax import lax
from jax.experimental import pallas as pl
from jax.experimental.pallas import tpu as pltpu
from jax.sharding import PartitionSpec as P

SKY = 32
CH = 32
F32 = jnp.float32
BF16 = jnp.bfloat16
HALF0 = [(0, y) for y in (0, 1, 2, 3)]
HALF1 = [(1, y) for y in (2, 3, 0, 1)]
OUT_POS = HALF0 + HALF1
IN_POS = (
    OUT_POS
    + [(-1, y) for y in (2, 3, 0, 1)]
    + [(2, y) for y in (0, 1, 2, 3)]
    + [(0, 4), (1, -1), (1, 4), (0, -1)]
    + [(2, 4), (-1, -1), (-1, 4), (2, -1)]
)


def dot(a, b, dims=((1,), (0,))):
    return lax.dot_general(a, b, (dims, ((), ())), preferred_element_type=F32)


def lane_block(shape):
    return lax.broadcasted_iota(jnp.int32, shape, len(shape) - 1) // CH


def split2(x):
    hi = x.astype(BF16)
    return hi, (x - hi.astype(F32)).astype(BF16)


def shift_rows(x, amount, group):
    row = lax.broadcasted_iota(jnp.int32, x.shape, 1)
    moved = pltpu.roll(x.astype(F32), amount % 16, axis=1)
    at = (row % group) - amount
    return jnp.where((at >= 0) & (at < group), moved, 0.0).astype(BF16)


def windows(hb):
    n = hb.shape[0]
    hb = hb.reshape(n, 2, 4, 16, 256)
    half0, half1 = hb[..., :128], hb[..., 128:]
    blk = lane_block((16, 128))[None, None, None]
    outer = jnp.broadcast_to((blk == 0) | (blk == 3), half0.shape)
    edge = jnp.where(outer, half0, half1)

    def shifted(part, amount, group):
        lead = part.shape[:-2]
        flat = part.reshape((-1, 16, 128))
        return shift_rows(flat, amount, group).reshape(lead + (16, 128))

    above = jnp.concatenate([shifted(edge[:, 1:2], 4, 16), edge[:, 0:1]], axis=1)
    below = jnp.concatenate([edge[:, 1:2], shifted(edge[:, 0:1], -4, 16)], axis=1)
    top = jnp.broadcast_to((blk == 1) | (blk == 3), half0.shape)
    rim = jnp.where(top, above, below)

    def from_left(part):
        return jnp.concatenate([shifted(part[:, :, 3:4], 1, 4), part[:, :, 0:3]], axis=2)

    def from_right(part):
        return jnp.concatenate([part[:, :, 1:4], shifted(part[:, :, 0:1], -1, 4)], axis=2)

    corner = jnp.where(outer, from_right(rim), from_left(rim))
    pieces = [half0, half1, from_left(half1), from_right(half0), rim, corner]
    return jnp.concatenate([p.reshape(n * 128, 128) for p in pieces], axis=1)


def network(
    own,
    reach,
    origin_ref,
    x_ref,
    keep_ref,
    lanes_ref,
    sw_ref,
    sb_ref,
    cw_ref,
    out_ref,
    h_ref,
    g_ref,
    w1_ref,
    w2_ref,
    k_ref,
    xs_ref,
    os_ref,
    perm_ref,
):
    wide = x_ref.shape[0]
    layers = sw_ref.shape[0]
    sides = (wide - own) // reach if reach else 0
    offset = origin_ref[0]

    p = lax.broadcasted_iota(jnp.int32, (1024, 1024), 0)
    y, x = p // SKY, p % SKY
    x2 = x % 2
    nb = x2 * 4 + ((y % 4) + 2 * x2) % 4
    r = (((y // 4) % 2) * 4 + (x // 2) % 4) * 16 + (y // 8) * 4 + x // 8
    q = lax.broadcasted_iota(jnp.int32, (1024, 1024), 1)
    perm_ref[...] = jnp.where(nb * 128 + r == q, 1.0, 0.0).astype(BF16)

    hi, lo = split2(x_ref[...])
    xp = dot(hi, perm_ref[...]) + dot(lo, perm_ref[...])
    for j in range(8):
        xs_ref[:, j, :] = xp[:, j * 128 : (j + 1) * 128]
    kp = dot(jnp.broadcast_to(keep_ref[...], (16, 1024)).astype(BF16), perm_ref[...])
    expand = jnp.where(
        lane_block((8, 256)) == lax.broadcasted_iota(jnp.int32, (8, 256), 0), 1.0, 0.0
    ).astype(BF16)
    k8 = jnp.concatenate([kp[0:1, j * 128 : (j + 1) * 128] for j in range(8)], axis=0)
    k_ref[...] = dot(k8.T.astype(BF16), expand).astype(BF16).reshape(8, 16, 256)

    lift_w, lift_b = lanes_ref[0:1, :], lanes_ref[1:2, :]

    def lift(f, _):
        hi, lo = split2(xs_ref[f].T)
        full = dot(hi, expand) + dot(lo, expand)
        fresh = (lift_w * full + lift_b).astype(BF16).reshape(8, 16, 256)
        h_ref[f] = fresh * k_ref[...]
        return 0

    lax.fori_loop(0, wide, lift, 0, unroll=4)
    g_ref[0] = jnp.zeros(g_ref.shape[1:], BF16)
    g_ref[wide + 1] = jnp.zeros(g_ref.shape[1:], BF16)

    spread = jnp.where(
        lax.broadcasted_iota(jnp.int32, (CH, 256), 1) % CH
        == lax.broadcasted_iota(jnp.int32, (CH, 256), 0),
        1.0,
        0.0,
    ).astype(BF16)
    block = lane_block((CH, 256))

    def layer_step(layer, _):
        taps = 0.5 * dot(sw_ref[layer].astype(F32).T.astype(BF16), spread)
        for kb, (xi, yi) in enumerate(IN_POS):
            rows = jnp.zeros((CH, 256), F32)
            for nb, (xo, yo) in enumerate(OUT_POS):
                a, b = yi - yo, xi - xo
                if abs(a) <= 1 and abs(b) <= 1:
                    tap = (a + 1) * 3 + b + 1
                    rows = jnp.where(block == nb, taps[tap * CH : (tap + 1) * CH], rows)
            w1_ref[kb * CH : (kb + 1) * CH, :] = rows.astype(BF16)
        taps = dot(cw_ref[layer].astype(F32).T.astype(BF16), spread)
        for kf in range(4):
            for kpos in range(4):
                rows = jnp.zeros((CH, 256), F32)
                for nf in range(2):
                    tap = kf - nf
                    if 0 <= tap <= 2:
                        rows = jnp.where(
                            block == nf * 4 + kpos, taps[tap * CH : (tap + 1) * CH], rows
                        )
                kb = kf * 4 + kpos
                w2_ref[kb * CH : (kb + 1) * CH, :] = rows.astype(BF16)
        bias = 0.5 * dot(sb_ref[layer], spread)[0:1]

        left = reach - layer if reach else 0
        count = own + sides * left
        count = count + count % 2
        start = jnp.minimum(jnp.maximum(offset - left, 0), wide - count)
        pairs = count // 2

        def gate(f):
            t = dot(windows(h_ref[pl.ds(f, 2)]), w1_ref[...]) + bias
            return (t + t * jnp.tanh(t)).astype(BF16).reshape(2, 8, 16, 256)

        def mix(f):
            gb = g_ref[pl.ds(f, 4)]
            halves = [
                jnp.concatenate(
                    [gb[k, :, :, s * 128 : (s + 1) * 128].reshape(128, 128) for k in range(4)],
                    axis=1,
                )
                for s in range(2)
            ]
            v = dot(jnp.concatenate(halves, axis=0), w2_ref[...])
            planes = [
                jnp.concatenate(
                    [v[s * 128 : (s + 1) * 128, n * 128 : (n + 1) * 128] for s in range(2)], axis=1
                )
                for n in range(2)
            ]
            v = jnp.stack(planes).reshape(2, 8, 16, 256)
            old = h_ref[pl.ds(f, 2)].astype(F32)
            return (0.5 * old + v).astype(BF16) * k_ref[...][None]

        def put_gate(i):
            f = start + 2 * i
            g_ref[pl.ds(f + 1, 2)] = gate(f)

        def put_mix(i):
            f = start + 2 * i
            h_ref[pl.ds(f, 2)] = mix(f)

        def both(i, _):
            f, f2 = start + 2 * i, start + 2 * i - 4
            new_h = mix(f2)
            new_g = gate(f)
            h_ref[pl.ds(f2, 2)] = new_h
            g_ref[pl.ds(f + 1, 2)] = new_g
            return 0

        put_gate(0)
        put_gate(1)
        lax.fori_loop(2, pairs, both, 0)
        put_mix(pairs - 2)
        put_mix(pairs - 1)
        return 0

    lax.fori_loop(0, layers, layer_step, 0)

    head = jnp.where(
        lane_block((8, 256)) == lax.broadcasted_iota(jnp.int32, (8, 256), 0), lanes_ref[2:3, :], 0.0
    )
    head_hi, head_lo = split2(head)
    heads = jnp.concatenate([head_hi.astype(F32), head_lo.astype(F32)], axis=0).astype(BF16)

    def score(f, _):
        both_parts = dot(heads, h_ref[offset + f].reshape(128, 256), ((1,), (1,)))
        os_ref[f] = both_parts[0:8] + both_parts[8:16]
        return 0

    lax.fori_loop(0, own, score, 0, unroll=4)
    tiled = jnp.concatenate([os_ref[:, j, :] for j in range(8)], axis=1)
    hi, lo = split2(tiled)
    back = ((1,), (1,))
    out_ref[...] = dot(hi, perm_ref[...], back) + dot(lo, perm_ref[...], back)


def run_network(own, reach, origin, x, keep, lanes, sw, sb, cw):
    wide = x.shape[0]
    vmem = pl.BlockSpec(memory_space=pltpu.VMEM)
    return pl.pallas_call(
        functools.partial(network, own, reach),
        out_shape=jax.ShapeDtypeStruct((own, 1024), F32),
        in_specs=[pl.BlockSpec(memory_space=pltpu.SMEM)] + [vmem] * 6,
        out_specs=vmem,
        scratch_shapes=[
            pltpu.VMEM((wide, 8, 16, 256), BF16),
            pltpu.VMEM((wide + 2, 8, 16, 256), BF16),
            pltpu.VMEM((768, 256), BF16),
            pltpu.VMEM((512, 256), BF16),
            pltpu.VMEM((8, 16, 256), BF16),
            pltpu.VMEM((wide, 8, 128), F32),
            pltpu.VMEM((own, 8, 128), F32),
            pltpu.VMEM((1024, 1024), BF16),
        ],
        compiler_params=pltpu.CompilerParams(vmem_limit_bytes=48 * 1024 * 1024),
    )(origin, x, keep, lanes, sw, sb, cw)


def per_device(
    cube,
    footprint,
    lift_weight,
    lift_bias,
    spatial_weight,
    spatial_bias,
    spectral_weight,
    head_weight,
):
    micro, planes, pixels = cube.shape
    segments = lax.axis_size("segment")
    tiles = lax.axis_size("tile")
    segment = lax.axis_index("segment")
    tile = lax.axis_index("tile")
    fields = micro // segments
    groups = tiles // fields
    own = planes * fields

    sw = lax.all_gather(spatial_weight, "segment", axis=0, tiled=True)
    sb = lax.all_gather(spatial_bias, "segment", axis=0, tiled=True)
    cw = lax.all_gather(spectral_weight, "segment", axis=0, tiled=True)
    layers = sw.shape[0]

    reach = layers if groups > 1 else 0
    wide = own + reach * min(2, groups - 1)
    mine = lax.dynamic_slice_in_dim(cube, segment * fields, fields, 0)
    whole = lax.all_to_all(
        jnp.concatenate([mine] * groups, axis=0), "tile", 0, 0, tiled=True
    ).reshape(tiles * planes, pixels)
    first = (tile // fields) * own
    begin = jnp.clip(first - reach, 0, tiles * planes - wide)
    x = lax.dynamic_slice_in_dim(whole, begin, wide, 0)
    keep = lax.dynamic_slice_in_dim(footprint, segment * fields + tile % fields, 1, 0).astype(F32)
    lanes = jnp.tile(jnp.stack([lift_weight, lift_bias, head_weight]), (1, 8))
    bias = jnp.broadcast_to(sb[:, None, :], (layers, 16, CH))
    out = run_network(
        own, reach, (first - begin).astype(jnp.int32)[None], x, keep, lanes, sw, bias, cw
    )
    cliques = [[g * fields + i for i in range(fields)] for g in range(groups)]
    return lax.all_to_all(
        out.reshape(fields, planes, pixels), "tile", 0, 0, axis_index_groups=cliques, tiled=True
    )


def solution(mesh):
    placed = (
        P(None, "tile", None),
        P(),
        P(),
        P(),
        P("segment", None, None),
        P("segment", None),
        P("segment", None, None),
        P(),
    )
    return jax.shard_map(
        per_device,
        mesh=mesh,
        in_specs=placed,
        out_specs=P("segment", "tile", None),
        check_vma=False,
    )
```

time: 703 us -> 130 us (0.18)
  other arithmetic: 177 us -> 1.63 us
  matrix products: 141 us -> 0 us
  waiting for transfers between devices: 138 us -> 0.01 us
  starting transfers between devices: 140 us -> 7.28 us
  Pallas kernels: 0 us -> 91 us
  local copies, waits for them, and re-layouts: 82.6 us -> 3.5 us
  blocking collectives: 17.6 us -> 26.1 us
    dot_general x132 -> x0, matrix products: 141 us -> none  [the longest x32 94.6 us: spatial_part(): jnp.einsum('oi,nip->nop', weight, stacked, preferred_element_type=jnp.flo...]
    while x160 -> x0, other arithmetic: 141 us -> none
    ppermute x64 -> x0, starting transfers between devices: 140 us -> none  [the longest x32 98.5 us: extended(): lax.ppermute(lax.slice_in_dim(block, block.shape[dim] - width, None, axis...]
    ppermute x64 -> x0, waiting for transfers between devices: 138 us -> none  [the longest x32 133 us: extended(): lax.ppermute(lax.slice_in_dim(block, 0, width, axis=dim), axis, backward)]
    pallas_call x0 -> x1, Pallas kernels: none -> 91 us  [run_network(): pl.pallas_call(functools.partial(network, own, reach), out_shape=jax.Shap...]
    while x168 -> x0, local copies, waits for them, and re-layouts: 70.1 us -> none
    concatenate x32 -> x1, other arithmetic: 28.6 us -> 0.85 us  [per_device(): jnp.concatenate([mine] * groups, axis=0)]
    all_to_all x0 -> x1, blocking collectives: none -> 10.2 us  [per_device(): lax.all_to_all(out.reshape(fields, planes, pixels), 'tile', 0, 0, axis_in...]
  transfers between devices with their start and end apart: 64 -> 1, of which waited for: 64 -> 0; matrix products, arithmetic and copies ran while one was open for 3% -> 1% of each run, Pallas kernels for 0% -> 0%
where the time goes in v1:
time: 130 us
  Pallas kernels  91 us (70%)
  blocking collectives  26.1 us (20%)
  starting transfers between devices  7.28 us (6%)
  local copies, waits for them, and re-layouts  3.5 us (3%)
  other arithmetic  1.63 us (1%)
    pallas_call x1, Pallas kernels, run_network(): pl.pallas_call(functools.partial(network, own, reach), out_shape=jax.Shap...  91 us
    all_to_all x1, blocking collectives, per_device(): lax.all_to_all(out.reshape(fields, planes, pixels), 'tile', 0, 0, axis_in...  10.2 us
    all_to_all x1, starting transfers between devices, per_device(): lax.all_to_all(jnp.concatenate([mine] * groups, axis=0), 'tile', 0, 0, ti...  7.28 us
    all_gather x1, blocking collectives, per_device(): sw = lax.all_gather(spatial_weight, 'segment', axis=0, tiled=True)  5.59 us
    all_gather x1, blocking collectives, per_device(): cw = lax.all_gather(spectral_weight, 'segment', axis=0, tiled=True)  5.23 us
    all_gather x1, blocking collectives, per_device(): sb = lax.all_gather(spatial_bias, 'segment', axis=0, tiled=True)  5.03 us
  transfers between devices with their start and end apart: 1, of which 0 were waited for; matrix products, arithmetic and copies ran while one was open for 1% of the time, Pallas kernels for 0%

profile of v1, /device:TPU:0, one launch (start us, length us, event | category | flops | bytes accessed | tf_op | source)
XLA Modules:
  0.0 129.6 jit_solution(9828313328332574983)
XLA Ops:
  0.0 0.0 copy-start
  0.0 1.1 copy-done
  1.2 0.1 copy.15
  1.3 0.9 pad_maximum_fusion
  2.2 7.3 %all-to-all-start = ((f32[8,12,1024]{2,1,0:T(8,128)}), f32[8,12,1024]{2,1,0:T(8,128)S(1)}, u32[]{:S(2)}, u32[]{:S(2)}) async-start(f32[8,12,1024]{2,1,0:T(8,128)} %pad_maximum_fusion), calls=%async_computation | async-start | bytes 1048576 | tf_op jit(solution)/shard_map/all_to_all | solution.py:286
  9.4 0.0 copy-start.3
  9.4 0.0 copy-start.4
  9.5 0.0 copy-start.5
  9.5 0.6 copy-done.3
  10.1 0.0 copy-done.4
  10.1 0.0 copy-done.5
  10.1 0.0 copy-start.6
  10.2 0.0 copy-start.2
  10.2 0.0 copy-start.1
  10.2 0.1 tile.10.lanes_ref
  10.3 0.5 copy-done.6
  10.8 5.0 %all-gather = bf16[4,2,32]{2,1,0:T(2,128)(2,1)S(1)} all-gather(bf16[1,2,32]{2,1,0:T(2,128)(2,1)S(1)} %bitcast.10), channel_id=1, replica_groups=mesh['tile'=8,'segment'=4] {'segment'}, dimensions={0}, use_global_device_ids=true | all-gather | bytes 640 | tf_op jit(solution)/shard_map/all_gather | solution.py:279
  15.8 0.0 copy-done.2
  15.8 5.2 %all_gather.11.cw_ref = bf16[8,32,96]{2,1,0:T(8,128)(2,1)S(1)} all-gather(bf16[2,32,96]{2,1,0:T(8,128)(2,1)S(1)} %copy-done.2), channel_id=1, replica_groups=mesh['tile'=8,'segment'=4] {'segment'}, dimensions={0}, use_global_device_ids=true | all-gather | bytes 61440 | tf_op jit(solution)/shard_map/all_gather | solution.py:280
  21.1 0.0 copy-done.1
  21.1 5.6 %all_gather.9.sw_ref = bf16[8,32,288]{2,1,0:T(8,128)(2,1)S(1)} all-gather(bf16[2,32,288]{2,1,0:T(8,128)(2,1)S(1)} %copy-done.1), channel_id=1, replica_groups=mesh['tile'=8,'segment'=4] {'segment'}, dimensions={0}, use_global_device_ids=true | all-gather | bytes 184320 | tf_op jit(solution)/shard_map/all_gather | solution.py:278
  26.7 0.8 dynamic-slice_convert_fusion.keep_ref
  27.4 0.0 all-to-all-done
  27.5 91.0 %shard_map.82 = f32[48,1024]{1,0:T(8,128)S(1)} custom-call(s32[1]{0:T(128)} %bitcast.origin_ref, f32[56,1024]{1,0:T(8,128)S(1)} %constant_dynamic-slice_fusion.x_ref, f32[1,1024]{1,0:T(1,128)S(1)} %dynamic-slice_convert_fusion.keep_ref, f32[3,256]{1,0:T(4,128)S(1)} %tile.10.lanes_ref, bf16[8,32,288]{2,1,0:T(8,128)(2,1)S(1)} %all_gather.9.sw_ref, ...), custom_call_target="tpu_custom_call" | custom-call | tf_op jit(solution)/shard_map/pallas_call | solution.py:240
  118.6 10.2 %all_to_all.10 = f32[4,12,1024]{2,1,0:T(8,128)S(1)} all-to-all(f32[4,12,1024]{2,1,0:T(8,128)S(1)} %reshape.12), channel_id=1, replica_groups={{0,4,8,12},{16,20,24,28},{1,5,9,13},{17,21,25,29},{2,6,10,14},{18,22,26..., dimensions={0} | all-to-all | bytes 393216 | tf_op jit(solution)/shard_map/all_to_all | solution.py:299
  128.8 0.8 copy.14
  (7 shorter events, 0.2 us)
Async XLA Ops:
  0.0 1.1 copy-start
  2.2 25.3 %all-to-all-start = ((f32[8,12,1024]{2,1,0:T(8,128)}), f32[8,12,1024]{2,1,0:T(8,128)S(1)}, u32[]{:S(2)}, u32[]{:S(2)}) async-start(f32[8,12,1024]{2,1,0:T(8,128)} %pad_maximum_fusion), calls=%async_computation | async-start | bytes 1048576 | tf_op jit(solution)/shard_map/all_to_all | solution.py:286
  9.4 0.7 copy-start.3
  9.4 0.7 copy-start.4
  9.5 0.7 copy-start.5
  10.1 0.7 copy-start.6
  10.2 5.7 %copy-start.2 = (bf16[2,32,96]{2,1,0:T(8,128)(2,1)S(1)}, bf16[2,32,96]{2,1,0:T(8,128)(2,1)}, u32[]{:S(2)}) copy-start(bf16[2,32,96]{2,1,0:T(8,128)(2,1)} %param.14) | copy-start | bytes 36868
  10.2 10.9 %copy-start.1 = (bf16[2,32,288]{2,1,0:T(8,128)(2,1)S(1)}, bf16[2,32,288]{2,1,0:T(8,128)(2,1)}, u32[]{:S(2)}) copy-start(bf16[2,32,288]{2,1,0:T(8,128)(2,1)} %param.12) | copy-start | bytes 110596

commit v2 on v1

--- a/solution.py
+++ b/solution.py
@@ -8,6 +8,7 @@
 from jax.sharding import PartitionSpec as P
 
 SKY = 32
+STEP = 4
 CH = 32
 F32 = jnp.float32
 BF16 = jnp.bfloat16
@@ -75,9 +76,10 @@
 def network(
     own,
     reach,
+    wide,
     origin_ref,
     x_ref,
-    keep_ref,
+    footprint_ref,
     lanes_ref,
     sw_ref,
     sb_ref,
@@ -92,10 +94,10 @@
     os_ref,
     perm_ref,
 ):
-    wide = x_ref.shape[0]
     layers = sw_ref.shape[0]
+    depth = sb_ref.shape[1]
     sides = (wide - own) // reach if reach else 0
-    offset = origin_ref[0]
+    offset, skip, member = origin_ref[0], origin_ref[1], origin_ref[2]
 
     p = lax.broadcasted_iota(jnp.int32, (1024, 1024), 0)
     y, x = p // SKY, p % SKY
@@ -105,11 +107,12 @@
     q = lax.broadcasted_iota(jnp.int32, (1024, 1024), 1)
     perm_ref[...] = jnp.where(nb * 128 + r == q, 1.0, 0.0).astype(BF16)
 
-    hi, lo = split2(x_ref[...])
+    hi, lo = split2(jnp.concatenate([x_ref[s] for s in range(x_ref.shape[0])], axis=0))
     xp = dot(hi, perm_ref[...]) + dot(lo, perm_ref[...])
     for j in range(8):
         xs_ref[:, j, :] = xp[:, j * 128 : (j + 1) * 128]
-    kp = dot(jnp.broadcast_to(keep_ref[...], (16, 1024)).astype(BF16), perm_ref[...])
+    keep = footprint_ref[pl.ds(member, 1), :].astype(F32)
+    kp = dot(jnp.broadcast_to(keep, (16, 1024)).astype(BF16), perm_ref[...])
     expand = jnp.where(
         lane_block((8, 256)) == lax.broadcasted_iota(jnp.int32, (8, 256), 0), 1.0, 0.0
     ).astype(BF16)
@@ -119,7 +122,7 @@
     lift_w, lift_b = lanes_ref[0:1, :], lanes_ref[1:2, :]
 
     def lift(f, _):
-        hi, lo = split2(xs_ref[f].T)
+        hi, lo = split2(xs_ref[skip + f].T)
         full = dot(hi, expand) + dot(lo, expand)
         fresh = (lift_w * full + lift_b).astype(BF16).reshape(8, 16, 256)
         h_ref[f] = fresh * k_ref[...]
@@ -159,59 +162,71 @@
                         )
                 kb = kf * 4 + kpos
                 w2_ref[kb * CH : (kb + 1) * CH, :] = rows.astype(BF16)
-        bias = 0.5 * dot(sb_ref[layer], spread)[0:1]
+        rows = sb_ref[layer // depth].astype(F32)
+        here = lax.broadcasted_iota(jnp.int32, rows.shape, 0) == layer % depth
+        row = jnp.sum(jnp.where(here, rows, 0.0), axis=0, keepdims=True)
+        bias = 0.5 * dot(jnp.broadcast_to(row, (16, CH)).astype(BF16), spread)[0:1]
 
         left = reach - layer if reach else 0
         count = own + sides * left
-        count = count + count % 2
+        count = (count + STEP - 1) // STEP * STEP
         start = jnp.minimum(jnp.maximum(offset - left, 0), wide - count)
-        pairs = count // 2
+        steps = count // STEP
 
         def gate(f):
-            t = dot(windows(h_ref[pl.ds(f, 2)]), w1_ref[...]) + bias
-            return (t + t * jnp.tanh(t)).astype(BF16).reshape(2, 8, 16, 256)
+            t = dot(windows(h_ref[pl.ds(f, STEP)]), w1_ref[...]) + bias
+            return (t + t * jnp.tanh(t)).astype(BF16).reshape(STEP, 8, 16, 256)
 
         def mix(f):
-            gb = g_ref[pl.ds(f, 4)]
+            gb = g_ref[pl.ds(f, STEP + 2)]
             halves = [
                 jnp.concatenate(
-                    [gb[k, :, :, s * 128 : (s + 1) * 128].reshape(128, 128) for k in range(4)],
+                    [
+                        gb[n + k, :, :, s * 128 : (s + 1) * 128].reshape(128, 128)
+                        for k in range(4)
+                    ],
                     axis=1,
                 )
+                for n in range(0, STEP, 2)
                 for s in range(2)
             ]
             v = dot(jnp.concatenate(halves, axis=0), w2_ref[...])
             planes = [
                 jnp.concatenate(
-                    [v[s * 128 : (s + 1) * 128, n * 128 : (n + 1) * 128] for s in range(2)], axis=1
+                    [
+                        v[(n + s) * 128 : (n + s + 1) * 128, m * 128 : (m + 1) * 128]
+                        for s in range(2)
+                    ],
+                    axis=1,
                 )
-                for n in range(2)
+                for n in range(0, STEP, 2)
+                for m in range(2)
             ]
-            v = jnp.stack(planes).reshape(2, 8, 16, 256)
-            old = h_ref[pl.ds(f, 2)].astype(F32)
+            v = jnp.stack(planes).reshape(STEP, 8, 16, 256)
+            old = h_ref[pl.ds(f, STEP)].astype(F32)
             return (0.5 * old + v).astype(BF16) * k_ref[...][None]
 
         def put_gate(i):
-            f = start + 2 * i
-            g_ref[pl.ds(f + 1, 2)] = gate(f)
+            f = start + STEP * i
+            g_ref[pl.ds(f + 1, STEP)] = gate(f)
 
         def put_mix(i):
-            f = start + 2 * i
-            h_ref[pl.ds(f, 2)] = mix(f)
+            f = start + STEP * i
+            h_ref[pl.ds(f, STEP)] = mix(f)
 
         def both(i, _):
-            f, f2 = start + 2 * i, start + 2 * i - 4
+            f, f2 = start + STEP * i, start + STEP * (i - 2)
             new_h = mix(f2)
             new_g = gate(f)
-            h_ref[pl.ds(f2, 2)] = new_h
-            g_ref[pl.ds(f + 1, 2)] = new_g
+            h_ref[pl.ds(f2, STEP)] = new_h
+            g_ref[pl.ds(f + 1, STEP)] = new_g
             return 0
 
         put_gate(0)
         put_gate(1)
-        lax.fori_loop(2, pairs, both, 0)
-        put_mix(pairs - 2)
-        put_mix(pairs - 1)
+        lax.fori_loop(2, steps, both, 0)
+        put_mix(steps - 2)
+        put_mix(steps - 1)
         return 0
 
     lax.fori_loop(0, layers, layer_step, 0)
@@ -231,15 +246,18 @@
     tiled = jnp.concatenate([os_ref[:, j, :] for j in range(8)], axis=1)
     hi, lo = split2(tiled)
     back = ((1,), (1,))
-    out_ref[...] = dot(hi, perm_ref[...], back) + dot(lo, perm_ref[...], back)
-
-
-def run_network(own, reach, origin, x, keep, lanes, sw, sb, cw):
-    wide = x.shape[0]
+    scores = dot(hi, perm_ref[...], back) + dot(lo, perm_ref[...], back)
+    planes = out_ref.shape[1]
+    for s in range(out_ref.shape[0]):
+        out_ref[s] = scores[s * planes : (s + 1) * planes]
+
+
+def run_network(own, reach, wide, origin, x, footprint, lanes, sw, sb, cw):
+    slots, planes = x.shape[:2]
     vmem = pl.BlockSpec(memory_space=pltpu.VMEM)
     return pl.pallas_call(
-        functools.partial(network, own, reach),
-        out_shape=jax.ShapeDtypeStruct((own, 1024), F32),
+        functools.partial(network, own, reach, wide),
+        out_shape=jax.ShapeDtypeStruct((own // planes, planes, 1024), F32),
         in_specs=[pl.BlockSpec(memory_space=pltpu.SMEM)] + [vmem] * 6,
         out_specs=vmem,
         scratch_shapes=[
@@ -248,12 +266,127 @@
             pltpu.VMEM((768, 256), BF16),
             pltpu.VMEM((512, 256), BF16),
             pltpu.VMEM((8, 16, 256), BF16),
-            pltpu.VMEM((wide, 8, 128), F32),
+            pltpu.VMEM((slots * planes, 8, 128), F32),
             pltpu.VMEM((own, 8, 128), F32),
             pltpu.VMEM((1024, 1024), BF16),
         ],
         compiler_params=pltpu.CompilerParams(vmem_limit_bytes=48 * 1024 * 1024),
-    )(origin, x, keep, lanes, sw, sb, cw)
+    )(origin, x, footprint, lanes, sw, sb, cw)
+
+
+MESH = pl.DeviceIdType.MESH
+
+
+def meet(peers):
+    barrier = pltpu.get_barrier_semaphore()
+    for peer in peers:
+        pl.semaphore_signal(barrier, inc=1, device_id=peer, device_id_type=MESH)
+    pl.semaphore_wait(barrier, len(peers))
+
+
+def slot_base(group, fields, slots, tiles):
+    return jnp.clip(group * fields - 1, 0, tiles - slots)
+
+
+def gather(fields, groups, *refs):
+    cube, parts, x_out, part_outs = refs[0], refs[1:4], refs[4], refs[5:8]
+    send_x, recv_x, send_w, recv_w, local = refs[8:]
+    slots = x_out.shape[0]
+    segments, tiles = part_outs[0].shape[0], fields * groups
+    tile, segment = lax.axis_index("tile"), lax.axis_index("segment")
+    group = tile // fields
+    base = slot_base(group, fields, slots, tiles)
+    mine = tile - base
+
+    def remote(src, dst, send, recv, peer):
+        return pltpu.make_async_remote_copy(
+            src_ref=src,
+            dst_ref=dst,
+            send_sem=send,
+            recv_sem=recv,
+            device_id=peer,
+            device_id_type=MESH,
+        )
+
+    others = [{"tile": (tile + k) % tiles} for k in range(1, tiles)]
+    across = [{"segment": (segment + k) % segments} for k in range(1, segments)]
+    meet(others + across)
+
+    def plane_copy(row, target, i):
+        other = target * fields + i
+        slot = tile - slot_base(target, fields, slots, tiles)
+        safe = jnp.clip(slot, 0, slots - 1)
+        wanted = (target >= 0) & (target < groups) & (slot >= 0) & (slot < slots)
+        copy = remote(
+            cube.at[segment * fields + i],
+            x_out.at[safe],
+            send_x.at[row, i],
+            recv_x.at[safe],
+            {"tile": jnp.clip(other, 0, tiles - 1)},
+        )
+        return wanted & (other != tile), copy
+
+    sends = [plane_copy(0, group, i) for i in range(fields)]
+    if groups > 1:
+        sends += [plane_copy(1, group + 1, i) for i in range(fields)]
+        sends += [plane_copy(2, group - 1, i) for i in range(fields)]
+    for wanted, copy in sends:
+        pl.when(wanted)(copy.start)
+    weights = [
+        remote(parts[a], part_outs[a].at[segment], send_w.at[a, k], recv_w.at[a, segment], peer)
+        for a in range(3)
+        for k, peer in enumerate(across)
+    ]
+    for copy in weights:
+        copy.start()
+    own = [pltpu.make_async_copy(cube.at[segment * fields + tile % fields], x_out.at[mine], local.at[3])]
+    own += [pltpu.make_async_copy(parts[a], part_outs[a].at[segment], local.at[a]) for a in range(3)]
+    for copy in own:
+        copy.start()
+
+    for slot in range(slots):
+        arriving = remote(cube.at[0], x_out.at[slot], send_x.at[0, 0], recv_x.at[slot], others[0])
+        pl.when(mine != slot)(arriving.wait_recv)
+    for a in range(3):
+        for k in range(1, segments):
+            source = (segment + k) % segments
+            remote(
+                parts[a], part_outs[a].at[source], send_w.at[a, 0], recv_w.at[a, source], across[0]
+            ).wait_recv()
+    for copy in own:
+        copy.wait()
+    for copy in weights:
+        copy.wait_send()
+    for wanted, copy in sends:
+        pl.when(wanted)(copy.wait_send)
+
+
+def scatter(fields, scores, out, send, recv, local):
+    tile = lax.axis_index("tile")
+    first, member = tile // fields * fields, tile % fields
+    peers = [(member + k) % fields for k in range(1, fields)]
+    meet([{"tile": first + peer} for peer in peers])
+
+    def copy_to(k, peer, slot):
+        return pltpu.make_async_remote_copy(
+            src_ref=scores.at[peer],
+            dst_ref=out.at[slot],
+            send_sem=send.at[k],
+            recv_sem=recv.at[slot],
+            device_id={"tile": first + peer},
+            device_id_type=MESH,
+        )
+
+    sends = [copy_to(k, peer, member) for k, peer in enumerate(peers)]
+    for copy in sends:
+        copy.start()
+    own = pltpu.make_async_copy(scores.at[member], out.at[member], local)
+    own.start()
+    for k, peer in enumerate(peers):
+        copy_to(k, peer, peer).wait_recv()
+    own.wait()
+    for copy in sends:
+        copy.wait_send()
 
 
 def per_device(
@@ -274,31 +407,56 @@
     fields = micro // segments
     groups = tiles // fields
     own = planes * fields
-
-    sw = lax.all_gather(spatial_weight, "segment", axis=0, tiled=True)
-    sb = lax.all_gather(spatial_bias, "segment", axis=0, tiled=True)
-    cw = lax.all_gather(spectral_weight, "segment", axis=0, tiled=True)
-    layers = sw.shape[0]
-
+    layers = spatial_weight.shape[0] * segments
     reach = layers if groups > 1 else 0
+    assert reach <= planes
     wide = own + reach * min(2, groups - 1)
-    mine = lax.dynamic_slice_in_dim(cube, segment * fields, fields, 0)
-    whole = lax.all_to_all(
-        jnp.concatenate([mine] * groups, axis=0), "tile", 0, 0, tiled=True
-    ).reshape(tiles * planes, pixels)
+    slots = fields + min(2, groups - 1)
+
+    hbm = pl.BlockSpec(memory_space=pl.ANY)
+    dma = pltpu.SemaphoreType.DMA
+    parts = (spatial_weight, spatial_bias, spectral_weight)
+    x, sw, sb, cw = pl.pallas_call(
+        functools.partial(gather, fields, groups),
+        out_shape=[jax.ShapeDtypeStruct((slots, planes, pixels), F32)]
+        + [jax.ShapeDtypeStruct((segments,) + part.shape, part.dtype) for part in parts],
+        in_specs=[hbm] * 4,
+        out_specs=[hbm] * 4,
+        scratch_shapes=[
+            dma((3, fields)),
+            dma((slots,)),
+            dma((3, segments)),
+            dma((3, segments)),
+            dma((4,)),
+        ],
+        compiler_params=pltpu.CompilerParams(collective_id=0, has_side_effects=True),
+    )(cube, *parts)
+
     first = (tile // fields) * own
     begin = jnp.clip(first - reach, 0, tiles * planes - wide)
-    x = lax.dynamic_slice_in_dim(whole, begin, wide, 0)
-    keep = lax.dynamic_slice_in_dim(footprint, segment * fields + tile % fields, 1, 0).astype(F32)
+    skip = begin - slot_base(tile // fields, fields, slots, tiles) * planes
+    origin = jnp.stack([first - begin, skip, segment * fields + tile % fields]).astype(jnp.int32)
     lanes = jnp.tile(jnp.stack([lift_weight, lift_bias, head_weight]), (1, 8))
-    bias = jnp.broadcast_to(sb[:, None, :], (layers, 16, CH))
-    out = run_network(
-        own, reach, (first - begin).astype(jnp.int32)[None], x, keep, lanes, sw, bias, cw
+    scores = run_network(
+        own,
+        reach,
+        wide,
+        origin,
+        x,
+        footprint,
+        lanes,
+        sw.reshape((layers,) + sw.shape[2:]),
+        sb,
+        cw.reshape((layers,) + cw.shape[2:]),
     )
-    cliques = [[g * fields + i for i in range(fields)] for g in range(groups)]
-    return lax.all_to_all(
-        out.reshape(fields, planes, pixels), "tile", 0, 0, axis_index_groups=cliques, tiled=True
-    )
+    return pl.pallas_call(
+        functools.partial(scatter, fields),
+        out_shape=jax.ShapeDtypeStruct((fields, planes, pixels), F32),
+        in_specs=[hbm],
+        out_specs=hbm,
+        scratch_shapes=[dma((fields,)), dma((fields,)), dma(())],
+        compiler_params=pltpu.CompilerParams(collective_id=1, has_side_effects=True),
+    )(scores)
 
 
 def solution(mesh):

time: 130 us -> 102 us (0.78)
  blocking collectives: 26.1 us -> 0 us
  starting transfers between devices: 7.28 us -> 0 us
  local copies, waits for them, and re-layouts: 3.5 us -> 9.1 us
  Pallas kernels: 91 us -> 92.9 us
  other arithmetic: 1.63 us -> 0.08 us
    all_gather x3 -> x0, blocking collectives: 15.8 us -> none  [the longest x1 5.59 us: per_device(): sw = lax.all_gather(spatial_weight, 'segment', axis=0, tiled=True)]
    all_to_all x1 -> x0, blocking collectives: 10.2 us -> none  [per_device(): lax.all_to_all(out.reshape(fields, planes, pixels), 'tile', 0, 0, axis_in...]
    all_to_all x1 -> x0, starting transfers between devices: 7.28 us -> none  [per_device(): lax.all_to_all(jnp.concatenate([mine] * groups, axis=0), 'tile', 0, 0, ti...]
    unnamed x15 -> x19, local copies, waits for them, and re-layouts: 2.47 us -> 7.26 us
    pallas_call x1 -> x3, Pallas kernels: 91 us -> 92.9 us  [the longest x1 73.5 us: run_network(): pl.pallas_call(functools.partial(network, own, reach, wide), out_shape=ja...]
    pallas_call x0 -> x1, local copies, waits for them, and re-layouts: none -> 1.76 us  [per_device(): pl.pallas_call(functools.partial(scatter, fields), out_shape=jax.ShapeDty...]
  transfers between devices with their start and end apart: 1 -> 0, of which waited for: 0 -> 0; matrix products, arithmetic and copies ran while one was open for 1% -> 0% of each run, Pallas kernels for 0% -> 0%
where the time goes in v2:
time: 102 us
  Pallas kernels  92.9 us (91%)
  local copies, waits for them, and re-layouts  9.1 us (9%)
    pallas_call x1, Pallas kernels, run_network(): pl.pallas_call(functools.partial(network, own, reach, wide), out_shape=ja...  73.5 us
    pallas_call x1, Pallas kernels, per_device(): pl.pallas_call(functools.partial(gather, fields, groups), out_shape=[jax....  12.1 us
    pallas_call x1, Pallas kernels, per_device(): pl.pallas_call(functools.partial(scatter, fields), out_shape=jax.ShapeDty...  7.32 us
    unnamed x19, local copies, waits for them, and re-layouts  7.26 us

profile of v2, /device:TPU:0, one launch (start us, length us, event | category | flops | bytes accessed | tf_op | source)
XLA Modules:
  0.0 102.1 jit_solution(1409691153167343495)
XLA Ops:
  0.0 0.1 pad_add_fusion.origin_ref
  0.1 2.6 %copy.9.refs_0_ = f32[16,12,1024]{2,1,0:T(8,128)} copy(f32[16,12,1024]{2,0,1:T(8,128)} %param.8) | data formatting | bytes 1572864 | tf_op args[0]
  2.6 0.0 copy-start.3
  2.6 12.1 %shard_map.82 = (f32[5,12,1024]{2,1,0:T(8,128)}, bf16[4,2,32,288]{3,2,1,0:T(8,128)(2,1)}, bf16[4,2,32]{2,1,0:T(2,128)(2,1)}, bf16[4,2,32,96]{3,2,1,0:T(8,128)(2,1)}) custom-call(f32[16,12,1024]{2,1,0:T(8,128)} %copy.9.refs_0_, bf16[2,32,288]{2,1,0:T(8,128)(2,1)} %refs_1_.1, bf16[2,32]{1,0:T(2,128)(2,1)} %refs_2_.1, bf16[2,32,96]{2,1,0:T(8,128)(2,1)} %refs_3_.1), custom_call_target="tpu_custom_call" | custom-call | tf_op jit(solution)/shard_map/pallas_call | solution.py:419
  14.7 0.0 copy-start.6
  14.7 0.0 copy-start.7
  14.7 0.0 copy-start.8
  14.8 0.6 copy-done.6
  15.4 0.0 copy-done.7
  15.4 0.0 copy-done.8
  15.4 0.0 copy-start.5
  15.4 0.1 tile.10.lanes_ref
  15.5 0.0 copy-done.3
  15.5 0.6 copy-done.5
  16.1 0.0 copy-start.1
  16.1 1.0 copy-done.1
  17.1 0.0 copy-start.2
  17.1 0.9 copy-done.2
  18.0 0.0 copy-start.4
  18.0 0.8 copy-done.4
  18.9 73.5 %shard_map.83.scores = f32[4,12,1024]{2,1,0:T(8,128)S(1)} custom-call(s32[3]{0:T(128)S(1)} %pad_add_fusion.origin_ref, f32[5,12,1024]{2,1,0:T(8,128)S(1)} %copy-done.1, s32[16,1024]{1,0:T(8,128)S(1)} %copy-done.3, f32[3,256]{1,0:T(4,128)S(1)} %tile.10.lanes_ref, bf16[8,32,288]{2,1,0:T(8,128)(2,1)S(1)} %bitcast.8, bf16[4,2,32]{2,1,0:T(2,128)(2,1)S(1)} %copy-done.5, ...), custom_call_target="tpu_custom_call" | custom-call | tf_op jit(solution)/shard_map/pallas_call | solution.py:258
  92.3 0.0 copy-start
  92.4 0.7 copy-done
  93.0 7.3 %shard_map.84 = f32[4,12,1024]{2,1,0:T(8,128)} custom-call(f32[4,12,1024]{2,1,0:T(8,128)} %copy-done), custom_call_target="tpu_custom_call" | custom-call | tf_op jit(solution)/shard_map/pallas_call | solution.py:452
  100.4 1.8 %copy.10 = f32[4,12,1024]{2,0,1:T(4,128)} copy(f32[4,12,1024]{2,1,0:T(8,128)} %shard_map.84) | data formatting | bytes 393216 | tf_op jit(solution)/shard_map/pallas_call | solution.py:452
  (2 shorter events, 0.0 us)
Async XLA Ops:
  2.6 12.9 %copy-start.3 = (s32[16,1024]{1,0:T(8,128)S(1)}, s32[16,1024]{1,0:T(8,128)}, u32[]{:S(2)}) copy-start(s32[16,1024]{1,0:T(8,128)} %footprint_ref.1) | copy-start | bytes 196612
  14.7 0.7 copy-start.6
  14.7 0.7 copy-start.7
  14.7 0.7 copy-start.8
  15.4 0.7 copy-start.5
  16.1 1.0 copy-start.1
  17.1 0.9 copy-start.2
  18.0 0.8 copy-start.4
  92.3 0.7 copy-start

commit v3 on v2

--- a/solution.py
+++ b/solution.py
@@ -78,12 +78,12 @@
     reach,
     wide,
     origin_ref,
-    x_ref,
     footprint_ref,
     lanes_ref,
-    sw_ref,
-    sb_ref,
-    cw_ref,
+    x_hbm,
+    sw_hbm,
+    sb_hbm,
+    cw_hbm,
     out_ref,
     h_ref,
     g_ref,
@@ -93,22 +93,37 @@
     xs_ref,
     os_ref,
     perm_ref,
+    x_ref,
+    sw_ref,
+    sb_ref,
+    cw_ref,
+    loaded,
 ):
+    loads = [
+        pltpu.make_async_copy(src, dst, loaded.at[n])
+        for n, (src, dst) in enumerate(
+            [(x_hbm, x_ref), (sw_hbm, sw_ref), (sb_hbm, sb_ref), (cw_hbm, cw_ref)]
+        )
+    ]
+    for load in loads:
+        load.start()
     layers = sw_ref.shape[0]
     depth = sb_ref.shape[1]
     sides = (wide - own) // reach if reach else 0
     offset, skip, member = origin_ref[0], origin_ref[1], origin_ref[2]
 
-    p = lax.broadcasted_iota(jnp.int32, (1024, 1024), 0)
-    y, x = p // SKY, p % SKY
-    x2 = x % 2
-    nb = x2 * 4 + ((y % 4) + 2 * x2) % 4
-    r = (((y // 4) % 2) * 4 + (x // 2) % 4) * 16 + (y // 8) * 4 + x // 8
-    q = lax.broadcasted_iota(jnp.int32, (1024, 1024), 1)
-    perm_ref[...] = jnp.where(nb * 128 + r == q, 1.0, 0.0).astype(BF16)
-
-    hi, lo = split2(jnp.concatenate([x_ref[s] for s in range(x_ref.shape[0])], axis=0))
-    xp = dot(hi, perm_ref[...]) + dot(lo, perm_ref[...])
+    q = lax.broadcasted_iota(jnp.int32, (8, 1024), 1)
+    nb, r = q // 128, q % 128
+    x2 = nb // 4
+    y = (r // 4) % 4 * 8 + r // 64 * 4 + (nb % 4 + 2 * x2) % 4
+    p = y * SKY + r % 4 * 8 + (r // 16) % 4 * 2 + x2
+    at = lax.broadcasted_iota(jnp.int32, (1024, 1024), 0)
+    perm_ref[...] = jnp.where(p[0:1] == at, 1.0, 0.0).astype(BF16)
+
+    for load in loads:
+        load.wait()
+    x = jnp.concatenate([x_ref[s].astype(F32) for s in range(x_ref.shape[0])], axis=0)
+    xp = dot(x.astype(BF16), perm_ref[...])
     for j in range(8):
         xs_ref[:, j, :] = xp[:, j * 128 : (j + 1) * 128]
     keep = footprint_ref[pl.ds(member, 1), :].astype(F32)
@@ -122,8 +137,7 @@
     lift_w, lift_b = lanes_ref[0:1, :], lanes_ref[1:2, :]
 
     def lift(f, _):
-        hi, lo = split2(xs_ref[skip + f].T)
-        full = dot(hi, expand) + dot(lo, expand)
+        full = dot(xs_ref[skip + f].T.astype(BF16), expand)
         fresh = (lift_w * full + lift_b).astype(BF16).reshape(8, 16, 256)
         h_ref[f] = fresh * k_ref[...]
         return 0
@@ -141,19 +155,19 @@
     block = lane_block((CH, 256))
 
     def layer_step(layer, _):
-        taps = 0.5 * dot(sw_ref[layer].astype(F32).T.astype(BF16), spread)
+        taps = (0.5 * dot(sw_ref[layer].astype(F32).T.astype(BF16), spread)).astype(BF16)
         for kb, (xi, yi) in enumerate(IN_POS):
-            rows = jnp.zeros((CH, 256), F32)
+            rows = jnp.zeros((CH, 256), BF16)
             for nb, (xo, yo) in enumerate(OUT_POS):
                 a, b = yi - yo, xi - xo
                 if abs(a) <= 1 and abs(b) <= 1:
                     tap = (a + 1) * 3 + b + 1
                     rows = jnp.where(block == nb, taps[tap * CH : (tap + 1) * CH], rows)
-            w1_ref[kb * CH : (kb + 1) * CH, :] = rows.astype(BF16)
-        taps = dot(cw_ref[layer].astype(F32).T.astype(BF16), spread)
+            w1_ref[kb * CH : (kb + 1) * CH, :] = rows
+        taps = dot(cw_ref[layer].astype(F32).T.astype(BF16), spread).astype(BF16)
         for kf in range(4):
             for kpos in range(4):
-                rows = jnp.zeros((CH, 256), F32)
+                rows = jnp.zeros((CH, 256), BF16)
                 for nf in range(2):
                     tap = kf - nf
                     if 0 <= tap <= 2:
@@ -161,7 +175,7 @@
                             block == nf * 4 + kpos, taps[tap * CH : (tap + 1) * CH], rows
                         )
                 kb = kf * 4 + kpos
-                w2_ref[kb * CH : (kb + 1) * CH, :] = rows.astype(BF16)
+                w2_ref[kb * CH : (kb + 1) * CH, :] = rows
         rows = sb_ref[layer // depth].astype(F32)
         here = lax.broadcasted_iota(jnp.int32, rows.shape, 0) == layer % depth
         row = jnp.sum(jnp.where(here, rows, 0.0), axis=0, keepdims=True)
@@ -174,8 +188,8 @@
         steps = count // STEP
 
         def gate(f):
-            t = dot(windows(h_ref[pl.ds(f, STEP)]), w1_ref[...]) + bias
-            return (t + t * jnp.tanh(t)).astype(BF16).reshape(STEP, 8, 16, 256)
+            t = (dot(windows(h_ref[pl.ds(f, STEP)]), w1_ref[...]) + bias).astype(BF16)
+            return (t + t * jnp.tanh(t)).reshape(STEP, 8, 16, 256)
 
         def mix(f):
             gb = g_ref[pl.ds(f, STEP + 2)]
@@ -202,9 +216,9 @@
                 for n in range(0, STEP, 2)
                 for m in range(2)
             ]
-            v = jnp.stack(planes).reshape(STEP, 8, 16, 256)
-            old = h_ref[pl.ds(f, STEP)].astype(F32)
-            return (0.5 * old + v).astype(BF16) * k_ref[...][None]
+            v = jnp.stack(planes).reshape(STEP, 8, 16, 256).astype(BF16)
+            half = jnp.asarray(0.5, BF16)
+            return (half * h_ref[pl.ds(f, STEP)] + v) * k_ref[...][None]
 
         def put_gate(i):
             f = start + STEP * i
@@ -244,21 +258,19 @@
 
     lax.fori_loop(0, own, score, 0, unroll=4)
     tiled = jnp.concatenate([os_ref[:, j, :] for j in range(8)], axis=1)
-    hi, lo = split2(tiled)
-    back = ((1,), (1,))
-    scores = dot(hi, perm_ref[...], back) + dot(lo, perm_ref[...], back)
+    scores = dot(tiled.astype(BF16), perm_ref[...], ((1,), (1,)))
     planes = out_ref.shape[1]
     for s in range(out_ref.shape[0]):
-        out_ref[s] = scores[s * planes : (s + 1) * planes]
+        out_ref[s] = scores[s * planes : (s + 1) * planes].astype(BF16)
 
 
 def run_network(own, reach, wide, origin, x, footprint, lanes, sw, sb, cw):
     slots, planes = x.shape[:2]
-    vmem = pl.BlockSpec(memory_space=pltpu.VMEM)
+    vmem, hbm = pl.BlockSpec(memory_space=pltpu.VMEM), pl.BlockSpec(memory_space=pl.ANY)
     return pl.pallas_call(
         functools.partial(network, own, reach, wide),
-        out_shape=jax.ShapeDtypeStruct((own // planes, planes, 1024), F32),
-        in_specs=[pl.BlockSpec(memory_space=pltpu.SMEM)] + [vmem] * 6,
+        out_shape=jax.ShapeDtypeStruct((own // planes, planes, 1024), BF16),
+        in_specs=[pl.BlockSpec(memory_space=pltpu.SMEM)] + [vmem] * 2 + [hbm] * 4,
         out_specs=vmem,
         scratch_shapes=[
             pltpu.VMEM((wide, 8, 16, 256), BF16),
@@ -269,9 +281,11 @@
             pltpu.VMEM((slots * planes, 8, 128), F32),
             pltpu.VMEM((own, 8, 128), F32),
             pltpu.VMEM((1024, 1024), BF16),
-        ],
+        ]
+        + [pltpu.VMEM(part.shape, part.dtype) for part in (x, sw, sb, cw)]
+        + [pltpu.SemaphoreType.DMA((4,))],
         compiler_params=pltpu.CompilerParams(vmem_limit_bytes=48 * 1024 * 1024),
-    )(origin, x, footprint, lanes, sw, sb, cw)
+    )(origin, footprint, lanes, x, sw, sb, cw)
 
 
 MESH = pl.DeviceIdType.MESH
@@ -318,7 +332,7 @@
         safe = jnp.clip(slot, 0, slots - 1)
         wanted = (target >= 0) & (target < groups) & (slot >= 0) & (slot < slots)
         copy = remote(
-            cube.at[segment * fields + i],
+            cube.at[i],
             x_out.at[safe],
             send_x.at[row, i],
             recv_x.at[safe],
@@ -339,7 +353,7 @@
     ]
     for copy in weights:
         copy.start()
-    own = [pltpu.make_async_copy(cube.at[segment * fields + tile % fields], x_out.at[mine], local.at[3])]
+    own = [pltpu.make_async_copy(cube.at[tile % fields], x_out.at[mine], local.at[3])]
     own += [pltpu.make_async_copy(parts[a], part_outs[a].at[segment], local.at[a]) for a in range(3)]
     for copy in own:
         copy.start()
@@ -415,10 +429,11 @@
 
     hbm = pl.BlockSpec(memory_space=pl.ANY)
     dma = pltpu.SemaphoreType.DMA
+    mine = lax.dynamic_slice_in_dim(cube, segment * fields, fields, 0).astype(BF16)
     parts = (spatial_weight, spatial_bias, spectral_weight)
     x, sw, sb, cw = pl.pallas_call(
         functools.partial(gather, fields, groups),
-        out_shape=[jax.ShapeDtypeStruct((slots, planes, pixels), F32)]
+        out_shape=[jax.ShapeDtypeStruct((slots, planes, pixels), BF16)]
         + [jax.ShapeDtypeStruct((segments,) + part.shape, part.dtype) for part in parts],
         in_specs=[hbm] * 4,
         out_specs=[hbm] * 4,
@@ -430,7 +445,7 @@
             dma((4,)),
         ],
         compiler_params=pltpu.CompilerParams(collective_id=0, has_side_effects=True),
-    )(cube, *parts)
+    )(mine, *parts)
 
     first = (tile // fields) * own
     begin = jnp.clip(first - reach, 0, tiles * planes - wide)
@@ -449,14 +464,15 @@
         sb,
         cw.reshape((layers,) + cw.shape[2:]),
     )
-    return pl.pallas_call(
+    mixed = pl.pallas_call(
         functools.partial(scatter, fields),
-        out_shape=jax.ShapeDtypeStruct((fields, planes, pixels), F32),
+        out_shape=jax.ShapeDtypeStruct((fields, planes, pixels), BF16),
         in_specs=[hbm],
         out_specs=hbm,
         scratch_shapes=[dma((fields,)), dma((fields,)), dma(())],
         compiler_params=pltpu.CompilerParams(collective_id=1, has_side_effects=True),
     )(scores)
+    return mixed.astype(F32)
 
 
 def solution(mesh):

time: 102 us -> 93.9 us (0.921)
  Pallas kernels: 92.9 us -> 85.3 us
    pallas_call x1, Pallas kernels: 73.5 us -> 68.7 us  [run_network(): pl.pallas_call(functools.partial(network, own, reach, wide), out_shape=ja...]
    pallas_call x1, Pallas kernels: 7.32 us -> 5.22 us  [per_device(): pl.pallas_call(functools.partial(scatter, fields), out_shape=jax.ShapeDty...]
    pallas_call x1 -> x0, local copies, waits for them, and re-layouts: 1.76 us -> none  [per_device(): pl.pallas_call(functools.partial(scatter, fields), out_shape=jax.ShapeDty...]
    convert_element_type x0 -> x1, local copies, waits for them, and re-layouts: none -> 1.66 us  [per_device(): return mixed.astype(F32)]
    unnamed x19 -> x21, local copies, waits for them, and re-layouts: 7.26 us -> 6.33 us
where the time goes in v3:
time: 93.9 us; the launch traced here: 93.6 us
  Pallas kernels  85.3 us (91%)
  local copies, waits for them, and re-layouts  8.12 us (9%)
    pallas_call x1, Pallas kernels, run_network(): pl.pallas_call(functools.partial(network, own, reach, wide), out_shape=ja...  68.7 us
    pallas_call x1, Pallas kernels, per_device(): pl.pallas_call(functools.partial(gather, fields, groups), out_shape=[jax....  11.3 us
    unnamed x21, local copies, waits for them, and re-layouts  6.33 us
    pallas_call x1, Pallas kernels, per_device(): pl.pallas_call(functools.partial(scatter, fields), out_shape=jax.ShapeDty...  5.22 us

profile of v3, /device:TPU:0, one launch (start us, length us, event | category | flops | bytes accessed | tf_op | source)
XLA Modules:
  0.0 93.6 jit_solution(4907145404033683071)
XLA Ops:
  0.0 0.0 copy-start
  0.0 0.1 pad_add_fusion.origin_ref
  0.1 1.1 %copy-done = f32[16,12,1024]{2,0,1:T(8,128)S(1)} copy-done((f32[16,12,1024]{2,0,1:T(8,128)S(1)}, f32[16,12,1024]{2,0,1:T(8,128)}, u32[]{:S(2)}) %copy-start) | copy-done | bytes 786456
  1.2 0.7 copy.13.refs_0_
  1.9 0.0 copy-start.4
  1.9 11.3 %shard_map.82 = (bf16[5,12,1024]{2,1,0:T(8,128)(2,1)}, bf16[4,2,32,288]{3,2,1,0:T(8,128)(2,1)}, bf16[4,2,32]{2,1,0:T(2,128)(2,1)}, bf16[4,2,32,96]{3,2,1,0:T(8,128)(2,1)}) custom-call(bf16[4,12,1024]{2,1,0:T(8,128)(2,1)} %copy.13.refs_0_, bf16[2,32,288]{2,1,0:T(8,128)(2,1)} %refs_1_.1, bf16[2,32]{1,0:T(2,128)(2,1)} %refs_2_.1, bf16[2,32,96]{2,1,0:T(8,128)(2,1)} %refs_3_.1), custom_call_target="tpu_custom_call" | custom-call | tf_op jit(solution)/shard_map/pallas_call | solution.py:434
  13.2 0.0 copy-start.7
  13.2 0.0 copy-start.8
  13.2 0.0 copy-start.9
  13.2 0.6 copy-done.7
  13.9 0.0 copy-done.8
  13.9 0.0 copy-done.9
  13.9 0.0 copy-start.6
  13.9 0.1 tile.10.lanes_ref
  14.0 0.0 copy-done.4
  14.0 0.6 copy-done.6
  14.6 0.0 copy-start.2
  14.6 0.9 copy-done.2
  15.5 0.0 copy-start.3
  15.5 0.9 copy-done.3
  16.4 0.0 copy-start.5
  16.4 0.8 copy-done.5
  17.3 68.7 %shard_map.83.scores = bf16[4,12,1024]{2,1,0:T(8,128)(2,1)S(1)} custom-call(s32[3]{0:T(128)S(1)} %pad_add_fusion.origin_ref, s32[16,1024]{1,0:T(8,128)S(1)} %copy-done.4, f32[3,256]{1,0:T(4,128)S(1)} %tile.10.lanes_ref, bf16[5,12,1024]{2,1,0:T(8,128)(2,1)S(1)} %copy-done.3, bf16[8,32,288]{2,1,0:T(8,128)(2,1)S(1)} %bitcast.8, ...), custom_call_target="tpu_custom_call" | custom-call | tf_op jit(solution)/shard_map/pallas_call | solution.py:270
  86.0 0.0 copy-start.1
  86.0 0.6 copy-done.1
  86.7 5.2 %shard_map.84 = bf16[4,12,1024]{2,1,0:T(8,128)(2,1)} custom-call(bf16[4,12,1024]{2,1,0:T(8,128)(2,1)} %copy-done.1), custom_call_target="tpu_custom_call" | custom-call | tf_op jit(solution)/shard_map/pallas_call | solution.py:467
  91.9 1.7 %copy.10 = f32[4,12,1024]{2,0,1:T(4,128)} copy(bf16[4,12,1024]{2,1,0:T(8,128)(2,1)} %shard_map.84) | data formatting | bytes 294912 | tf_op jit(solution)/shard_map/convert_element_type | solution.py:475
  (3 shorter events, 0.1 us)
Async XLA Ops:
  0.0 1.1 %copy-start = (f32[16,12,1024]{2,0,1:T(8,128)S(1)}, f32[16,12,1024]{2,0,1:T(8,128)}, u32[]{:S(2)}) copy-start(f32[16,12,1024]{2,0,1:T(8,128)} %param.8) | copy-start | bytes 2359300
  1.9 12.1 %copy-start.4 = (s32[16,1024]{1,0:T(8,128)S(1)}, s32[16,1024]{1,0:T(8,128)}, u32[]{:S(2)}) copy-start(s32[16,1024]{1,0:T(8,128)} %footprint_ref.1) | copy-start | bytes 196612
  13.2 0.7 copy-start.7
  13.2 0.7 copy-start.8
  13.2 0.7 copy-start.9
  13.9 0.7 copy-start.6
  14.6 0.9 copy-start.2
  15.5 0.9 copy-start.3
  16.4 0.8 copy-start.5
  86.0 0.7 copy-start.1

commit v4 on v3

--- a/solution.py
+++ b/solution.py
@@ -8,7 +8,7 @@
 from jax.sharding import PartitionSpec as P
 
 SKY = 32
-STEP = 4
+STEP = 8
 CH = 32
 F32 = jnp.float32
 BF16 = jnp.bfloat16
@@ -80,10 +80,10 @@
     origin_ref,
     footprint_ref,
     lanes_ref,
-    x_hbm,
-    sw_hbm,
-    sb_hbm,
-    cw_hbm,
+    x_ref,
+    sw_ref,
+    sb_ref,
+    cw_ref,
     out_ref,
     h_ref,
     g_ref,
@@ -93,20 +93,7 @@
     xs_ref,
     os_ref,
     perm_ref,
-    x_ref,
-    sw_ref,
-    sb_ref,
-    cw_ref,
-    loaded,
 ):
-    loads = [
-        pltpu.make_async_copy(src, dst, loaded.at[n])
-        for n, (src, dst) in enumerate(
-            [(x_hbm, x_ref), (sw_hbm, sw_ref), (sb_hbm, sb_ref), (cw_hbm, cw_ref)]
-        )
-    ]
-    for load in loads:
-        load.start()
     layers = sw_ref.shape[0]
     depth = sb_ref.shape[1]
     sides = (wide - own) // reach if reach else 0
@@ -120,8 +107,6 @@
     at = lax.broadcasted_iota(jnp.int32, (1024, 1024), 0)
     perm_ref[...] = jnp.where(p[0:1] == at, 1.0, 0.0).astype(BF16)
 
-    for load in loads:
-        load.wait()
     x = jnp.concatenate([x_ref[s].astype(F32) for s in range(x_ref.shape[0])], axis=0)
     xp = dot(x.astype(BF16), perm_ref[...])
     for j in range(8):
@@ -266,11 +251,11 @@
 
 def run_network(own, reach, wide, origin, x, footprint, lanes, sw, sb, cw):
     slots, planes = x.shape[:2]
-    vmem, hbm = pl.BlockSpec(memory_space=pltpu.VMEM), pl.BlockSpec(memory_space=pl.ANY)
+    vmem = pl.BlockSpec(memory_space=pltpu.VMEM)
     return pl.pallas_call(
         functools.partial(network, own, reach, wide),
         out_shape=jax.ShapeDtypeStruct((own // planes, planes, 1024), BF16),
-        in_specs=[pl.BlockSpec(memory_space=pltpu.SMEM)] + [vmem] * 2 + [hbm] * 4,
+        in_specs=[pl.BlockSpec(memory_space=pltpu.SMEM)] + [vmem] * 6,
         out_specs=vmem,
         scratch_shapes=[
             pltpu.VMEM((wide, 8, 16, 256), BF16),
@@ -281,9 +266,7 @@
             pltpu.VMEM((slots * planes, 8, 128), F32),
             pltpu.VMEM((own, 8, 128), F32),
             pltpu.VMEM((1024, 1024), BF16),
-        ]
-        + [pltpu.VMEM(part.shape, part.dtype) for part in (x, sw, sb, cw)]
-        + [pltpu.SemaphoreType.DMA((4,))],
+        ],
         compiler_params=pltpu.CompilerParams(vmem_limit_bytes=48 * 1024 * 1024),
     )(origin, footprint, lanes, x, sw, sb, cw)
 
@@ -427,7 +410,7 @@
     wide = own + reach * min(2, groups - 1)
     slots = fields + min(2, groups - 1)
 
-    hbm = pl.BlockSpec(memory_space=pl.ANY)
+    hbm, vmem = pl.BlockSpec(memory_space=pl.ANY), pl.BlockSpec(memory_space=pltpu.VMEM)
     dma = pltpu.SemaphoreType.DMA
     mine = lax.dynamic_slice_in_dim(cube, segment * fields, fields, 0).astype(BF16)
     parts = (spatial_weight, spatial_bias, spectral_weight)
@@ -435,8 +418,8 @@
         functools.partial(gather, fields, groups),
         out_shape=[jax.ShapeDtypeStruct((slots, planes, pixels), BF16)]
         + [jax.ShapeDtypeStruct((segments,) + part.shape, part.dtype) for part in parts],
-        in_specs=[hbm] * 4,
-        out_specs=[hbm] * 4,
+        in_specs=[vmem] + [hbm] * 3,
+        out_specs=[vmem] * 4,
         scratch_shapes=[
             dma((3, fields)),
             dma((slots,)),
@@ -467,8 +450,8 @@
     mixed = pl.pallas_call(
         functools.partial(scatter, fields),
         out_shape=jax.ShapeDtypeStruct((fields, planes, pixels), BF16),
-        in_specs=[hbm],
-        out_specs=hbm,
+        in_specs=[vmem],
+        out_specs=vmem,
         scratch_shapes=[dma((fields,)), dma((fields,)), dma(())],
         compiler_params=pltpu.CompilerParams(collective_id=1, has_side_effects=True),
     )(scores)

time: 93.9 us -> 89.4 us (0.952)
  Pallas kernels: 85.3 us -> 80.8 us
    pallas_call x1, Pallas kernels: 68.7 us -> 61.4 us  [run_network(): pl.pallas_call(functools.partial(network, own, reach, wide), out_shape=ja...]
    pallas_call x1, Pallas kernels: 11.3 us -> 12.9 us  [per_device(): pl.pallas_call(functools.partial(gather, fields, groups), out_shape=[jax....]
    pallas_call x1, Pallas kernels: 5.22 us -> 6.45 us  [per_device(): pl.pallas_call(functools.partial(scatter, fields), out_shape=jax.ShapeDty...]
where the time goes in v4:
time: 89.4 us; the launch traced here: 89.1 us
  Pallas kernels  80.8 us (90%)
  local copies, waits for them, and re-layouts  8.12 us (9%)
    pallas_call x1, Pallas kernels, run_network(): pl.pallas_call(functools.partial(network, own, reach, wide), out_shape=ja...  61.4 us
    pallas_call x1, Pallas kernels, per_device(): pl.pallas_call(functools.partial(gather, fields, groups), out_shape=[jax....  12.9 us
    pallas_call x1, Pallas kernels, per_device(): pl.pallas_call(functools.partial(scatter, fields), out_shape=jax.ShapeDty...  6.45 us
    unnamed x21, local copies, waits for them, and re-layouts  6.33 us

profile of v4, /device:TPU:0, one launch (start us, length us, event | category | flops | bytes accessed | tf_op | source)
XLA Modules:
  0.0 89.1 jit_solution(15068536815237230052)
XLA Ops:
  0.0 0.0 copy-start
  0.0 0.1 pad_add_fusion.origin_ref
  0.1 1.1 %copy-done = f32[16,12,1024]{2,0,1:T(8,128)S(1)} copy-done((f32[16,12,1024]{2,0,1:T(8,128)S(1)}, f32[16,12,1024]{2,0,1:T(8,128)}, u32[]{:S(2)}) %copy-start) | copy-done | bytes 786456
  1.2 0.7 copy.13.refs_0_
  1.9 0.0 copy-start.4
  1.9 12.9 %shard_map.82 = (bf16[5,12,1024]{2,1,0:T(8,128)(2,1)}, bf16[4,2,32,288]{3,2,1,0:T(8,128)(2,1)}, bf16[4,2,32]{2,1,0:T(2,128)(2,1)}, bf16[4,2,32,96]{3,2,1,0:T(8,128)(2,1)}) custom-call(bf16[4,12,1024]{2,1,0:T(8,128)(2,1)} %copy.13.refs_0_, bf16[2,32,288]{2,1,0:T(8,128)(2,1)} %refs_1_.1, bf16[2,32]{1,0:T(2,128)(2,1)} %refs_2_.1, bf16[2,32,96]{2,1,0:T(8,128)(2,1)} %refs_3_.1), custom_call_target="tpu_custom_call" | custom-call | tf_op jit(solution)/shard_map/pallas_call | solution.py:417
  14.8 0.0 copy-start.7
  14.8 0.0 copy-start.8
  14.8 0.0 copy-start.9
  14.8 0.6 copy-done.7
  15.4 0.0 copy-done.8
  15.5 0.0 copy-done.9
  15.5 0.0 copy-start.6
  15.5 0.1 tile.10.lanes_ref
  15.6 0.0 copy-done.4
  15.6 0.6 copy-done.6
  16.2 0.0 copy-start.2
  16.2 0.9 %copy-done.2 = bf16[4,2,32,288]{3,2,1,0:T(8,128)(2,1)S(1)} copy-done((bf16[4,2,32,288]{3,2,1,0:T(8,128)(2,1)S(1)}, bf16[4,2,32,288]{3,2,1,0:T(8,128)(2,1)}, u32[]{:S(2)}) %copy-start.2) | copy-done | bytes 147480
  17.1 0.0 copy-start.3
  17.1 0.9 %copy-done.3 = bf16[5,12,1024]{2,1,0:T(8,128)(2,1)S(1)} copy-done((bf16[5,12,1024]{2,1,0:T(8,128)(2,1)S(1)}, bf16[5,12,1024]{2,1,0:T(8,128)(2,1)}, u32[]{:S(2)}) %copy-start.3) | copy-done | bytes 122904
  18.0 0.0 copy-start.5
  18.0 0.8 copy-done.5
  18.8 61.4 %shard_map.83.scores = bf16[4,12,1024]{2,1,0:T(8,128)(2,1)S(1)} custom-call(s32[3]{0:T(128)S(1)} %pad_add_fusion.origin_ref, s32[16,1024]{1,0:T(8,128)S(1)} %copy-done.4, f32[3,256]{1,0:T(4,128)S(1)} %tile.10.lanes_ref, bf16[5,12,1024]{2,1,0:T(8,128)(2,1)S(1)} %copy-done.3, bf16[8,32,288]{2,1,0:T(8,128)(2,1)S(1)} %bitcast.8, ...), custom_call_target="tpu_custom_call" | custom-call | tf_op jit(solution)/shard_map/pallas_call | solution.py:255
  80.3 0.0 copy-start.1
  80.3 0.6 copy-done.1
  81.0 6.4 %shard_map.84 = bf16[4,12,1024]{2,1,0:T(8,128)(2,1)} custom-call(bf16[4,12,1024]{2,1,0:T(8,128)(2,1)} %copy-done.1), custom_call_target="tpu_custom_call" | custom-call | tf_op jit(solution)/shard_map/pallas_call | solution.py:450
  87.4 1.7 %copy.10 = f32[4,12,1024]{2,0,1:T(4,128)} copy(bf16[4,12,1024]{2,1,0:T(8,128)(2,1)} %shard_map.84) | data formatting | bytes 294912 | tf_op jit(solution)/shard_map/convert_element_type | solution.py:458
  (3 shorter events, 0.1 us)
Async XLA Ops:
  0.0 1.1 %copy-start = (f32[16,12,1024]{2,0,1:T(8,128)S(1)}, f32[16,12,1024]{2,0,1:T(8,128)}, u32[]{:S(2)}) copy-start(f32[16,12,1024]{2,0,1:T(8,128)} %param.8) | copy-start | bytes 2359300
  1.9 13.7 %copy-start.4 = (s32[16,1024]{1,0:T(8,128)S(1)}, s32[16,1024]{1,0:T(8,128)}, u32[]{:S(2)}) copy-start(s32[16,1024]{1,0:T(8,128)} %footprint_ref.1) | copy-start | bytes 196612
  14.8 0.7 copy-start.7
  14.8 0.7 copy-start.8
  14.8 0.7 copy-start.9
  15.5 0.7 copy-start.6
  16.2 0.9 %copy-start.2 = (bf16[4,2,32,288]{3,2,1,0:T(8,128)(2,1)S(1)}, bf16[4,2,32,288]{3,2,1,0:T(8,128)(2,1)}, u32[]{:S(2)}) copy-start(bf16[4,2,32,288]{3,2,1,0:T(8,128)(2,1)} %get-tuple-element.10) | copy-start | bytes 442372
  17.1 0.9 %copy-start.3 = (bf16[5,12,1024]{2,1,0:T(8,128)(2,1)S(1)}, bf16[5,12,1024]{2,1,0:T(8,128)(2,1)}, u32[]{:S(2)}) copy-start(bf16[5,12,1024]{2,1,0:T(8,128)(2,1)} %get-tuple-element.9.x_ref) | copy-start | bytes 368644
  18.0 0.8 copy-start.5
  80.3 0.7 copy-start.1

commit v5 on v3

--- a/solution.py
+++ b/solution.py
@@ -8,7 +8,7 @@
 from jax.sharding import PartitionSpec as P
 
 SKY = 32
-STEP = 4
+STEP = 8
 CH = 32
 F32 = jnp.float32
 BF16 = jnp.bfloat16
@@ -266,11 +266,12 @@
 
 def run_network(own, reach, wide, origin, x, footprint, lanes, sw, sb, cw):
     slots, planes = x.shape[:2]
-    vmem, hbm = pl.BlockSpec(memory_space=pltpu.VMEM), pl.BlockSpec(memory_space=pl.ANY)
+    vmem = pl.BlockSpec(memory_space=pltpu.VMEM)
+    far = pl.BlockSpec(memory_space=pltpu.HBM)
     return pl.pallas_call(
         functools.partial(network, own, reach, wide),
         out_shape=jax.ShapeDtypeStruct((own // planes, planes, 1024), BF16),
-        in_specs=[pl.BlockSpec(memory_space=pltpu.SMEM)] + [vmem] * 2 + [hbm] * 4,
+        in_specs=[pl.BlockSpec(memory_space=pltpu.SMEM)] + [vmem] * 2 + [far] * 4,
         out_specs=vmem,
         scratch_shapes=[
             pltpu.VMEM((wide, 8, 16, 256), BF16),
@@ -427,7 +428,7 @@
     wide = own + reach * min(2, groups - 1)
     slots = fields + min(2, groups - 1)
 
-    hbm = pl.BlockSpec(memory_space=pl.ANY)
+    hbm, vmem = pl.BlockSpec(memory_space=pl.ANY), pl.BlockSpec(memory_space=pltpu.VMEM)
     dma = pltpu.SemaphoreType.DMA
     mine = lax.dynamic_slice_in_dim(cube, segment * fields, fields, 0).astype(BF16)
     parts = (spatial_weight, spatial_bias, spectral_weight)
@@ -435,7 +436,7 @@
         functools.partial(gather, fields, groups),
         out_shape=[jax.ShapeDtypeStruct((slots, planes, pixels), BF16)]
         + [jax.ShapeDtypeStruct((segments,) + part.shape, part.dtype) for part in parts],
-        in_specs=[hbm] * 4,
+        in_specs=[vmem] + [hbm] * 3,
         out_specs=[hbm] * 4,
         scratch_shapes=[
             dma((3, fields)),
@@ -467,8 +468,8 @@
     mixed = pl.pallas_call(
         functools.partial(scatter, fields),
         out_shape=jax.ShapeDtypeStruct((fields, planes, pixels), BF16),
-        in_specs=[hbm],
-        out_specs=hbm,
+        in_specs=[vmem],
+        out_specs=vmem,
         scratch_shapes=[dma((fields,)), dma((fields,)), dma(())],
         compiler_params=pltpu.CompilerParams(collective_id=1, has_side_effects=True),
     )(scores)

time: 93.9 us -> 89.6 us (0.954)
  Pallas kernels: 85.3 us -> 81 us
    pallas_call x1, Pallas kernels: 68.7 us -> 62.3 us  [run_network(): pl.pallas_call(functools.partial(network, own, reach, wide), out_shape=ja...]
    pallas_call x1, Pallas kernels: 5.22 us -> 6.45 us  [per_device(): pl.pallas_call(functools.partial(scatter, fields), out_shape=jax.ShapeDty...]
    pallas_call x1, Pallas kernels: 11.3 us -> 12.3 us  [per_device(): pl.pallas_call(functools.partial(gather, fields, groups), out_shape=[jax....]
where the time goes in v5:
time: 89.6 us; the launch traced here: 89.3 us
  Pallas kernels  81 us (90%)
  local copies, waits for them, and re-layouts  8.12 us (9%)
    pallas_call x1, Pallas kernels, run_network(): pl.pallas_call(functools.partial(network, own, reach, wide), out_shape=ja...  62.3 us
    pallas_call x1, Pallas kernels, per_device(): pl.pallas_call(functools.partial(gather, fields, groups), out_shape=[jax....  12.3 us
    pallas_call x1, Pallas kernels, per_device(): pl.pallas_call(functools.partial(scatter, fields), out_shape=jax.ShapeDty...  6.45 us
    unnamed x21, local copies, waits for them, and re-layouts  6.33 us

profile of v5, /device:TPU:0, one launch (start us, length us, event | category | flops | bytes accessed | tf_op | source)
XLA Modules:
  0.0 89.3 jit_solution(9717837678436760442)
XLA Ops:
  0.0 0.0 copy-start
  0.0 0.1 pad_add_fusion.origin_ref
  0.1 1.1 %copy-done = f32[16,12,1024]{2,0,1:T(8,128)S(1)} copy-done((f32[16,12,1024]{2,0,1:T(8,128)S(1)}, f32[16,12,1024]{2,0,1:T(8,128)}, u32[]{:S(2)}) %copy-start) | copy-done | bytes 786456
  1.2 0.7 copy.13.refs_0_
  1.9 0.0 copy-start.4
  1.9 12.3 %shard_map.82 = (bf16[5,12,1024]{2,1,0:T(8,128)(2,1)}, bf16[4,2,32,288]{3,2,1,0:T(8,128)(2,1)}, bf16[4,2,32]{2,1,0:T(2,128)(2,1)}, bf16[4,2,32,96]{3,2,1,0:T(8,128)(2,1)}) custom-call(bf16[4,12,1024]{2,1,0:T(8,128)(2,1)} %copy.13.refs_0_, bf16[2,32,288]{2,1,0:T(8,128)(2,1)} %refs_1_.1, bf16[2,32]{1,0:T(2,128)(2,1)} %refs_2_.1, bf16[2,32,96]{2,1,0:T(8,128)(2,1)} %refs_3_.1), custom_call_target="tpu_custom_call" | custom-call | tf_op jit(solution)/shard_map/pallas_call | solution.py:435
  14.1 0.0 copy-start.7
  14.2 0.0 copy-start.8
  14.2 0.0 copy-start.9
  14.2 0.6 copy-done.7
  14.8 0.0 copy-done.8
  14.8 0.0 copy-done.9
  14.9 0.0 copy-start.6
  14.9 0.1 tile.10.lanes_ref
  14.9 0.0 copy-done.4
  14.9 0.6 copy-done.6
  15.5 0.0 copy-start.2
  15.5 0.9 %copy-done.2 = bf16[4,2,32,288]{3,2,1,0:T(8,128)(2,1)S(1)} copy-done((bf16[4,2,32,288]{3,2,1,0:T(8,128)(2,1)S(1)}, bf16[4,2,32,288]{3,2,1,0:T(8,128)(2,1)}, u32[]{:S(2)}) %copy-start.2) | copy-done | bytes 147480
  16.5 0.0 copy-start.3
  16.5 0.9 %copy-done.3 = bf16[5,12,1024]{2,1,0:T(8,128)(2,1)S(1)} copy-done((bf16[5,12,1024]{2,1,0:T(8,128)(2,1)S(1)}, bf16[5,12,1024]{2,1,0:T(8,128)(2,1)}, u32[]{:S(2)}) %copy-start.3) | copy-done | bytes 122904
  17.4 0.0 copy-start.5
  17.4 0.8 copy-done.5
  18.2 62.3 %shard_map.83.scores = bf16[4,12,1024]{2,1,0:T(8,128)(2,1)S(1)} custom-call(s32[3]{0:T(128)S(1)} %pad_add_fusion.origin_ref, s32[16,1024]{1,0:T(8,128)S(1)} %copy-done.4, f32[3,256]{1,0:T(4,128)S(1)} %tile.10.lanes_ref, bf16[5,12,1024]{2,1,0:T(8,128)(2,1)S(1)} %copy-done.3, bf16[8,32,288]{2,1,0:T(8,128)(2,1)S(1)} %bitcast.8, ...), custom_call_target="tpu_custom_call" | custom-call | tf_op jit(solution)/shard_map/pallas_call | solution.py:271
  80.5 0.0 copy-start.1
  80.5 0.6 copy-done.1
  81.1 6.4 %shard_map.84 = bf16[4,12,1024]{2,1,0:T(8,128)(2,1)} custom-call(bf16[4,12,1024]{2,1,0:T(8,128)(2,1)} %copy-done.1), custom_call_target="tpu_custom_call" | custom-call | tf_op jit(solution)/shard_map/pallas_call | solution.py:468
  87.6 1.7 %copy.10 = f32[4,12,1024]{2,0,1:T(4,128)} copy(bf16[4,12,1024]{2,1,0:T(8,128)(2,1)} %shard_map.84) | data formatting | bytes 294912 | tf_op jit(solution)/shard_map/convert_element_type | solution.py:476
  (3 shorter events, 0.1 us)
Async XLA Ops:
  0.0 1.1 %copy-start = (f32[16,12,1024]{2,0,1:T(8,128)S(1)}, f32[16,12,1024]{2,0,1:T(8,128)}, u32[]{:S(2)}) copy-start(f32[16,12,1024]{2,0,1:T(8,128)} %param.8) | copy-start | bytes 2359300
  1.9 13.1 %copy-start.4 = (s32[16,1024]{1,0:T(8,128)S(1)}, s32[16,1024]{1,0:T(8,128)}, u32[]{:S(2)}) copy-start(s32[16,1024]{1,0:T(8,128)} %footprint_ref.1) | copy-start | bytes 196612
  14.1 0.7 copy-start.7
  14.2 0.7 copy-start.8
  14.2 0.7 copy-start.9
  14.9 0.7 copy-start.6
  15.5 0.9 %copy-start.2 = (bf16[4,2,32,288]{3,2,1,0:T(8,128)(2,1)S(1)}, bf16[4,2,32,288]{3,2,1,0:T(8,128)(2,1)}, u32[]{:S(2)}) copy-start(bf16[4,2,32,288]{3,2,1,0:T(8,128)(2,1)} %get-tuple-element.10) | copy-start | bytes 442372
  16.5 0.9 %copy-start.3 = (bf16[5,12,1024]{2,1,0:T(8,128)(2,1)S(1)}, bf16[5,12,1024]{2,1,0:T(8,128)(2,1)}, u32[]{:S(2)}) copy-start(bf16[5,12,1024]{2,1,0:T(8,128)(2,1)} %get-tuple-element.9.x_hbm) | copy-start | bytes 368644
  17.4 0.8 copy-start.5
  80.5 0.7 copy-start.1
